TPU v7x, 256 devices: a whole 4x4x8 slice. The times are simulated.
256 devices in a mesh: row: 8 (over y_lo, x), col: 32 (over y_hi, z, core).
Axes of the slice: x: 4, y: 4 (y_hi: 2, y_lo: 2; y = y_hi * 2 + y_lo), z: 8, core: 2. Of those that a mesh axis runs over, the one named last changes fastest.
Arguments:
- ampl: bfloat16 [1792, 256, 1792], P('col', 'row'), may hold values from -0.015625 to 0.015625
- integrals: bfloat16 [1024, 256, 1792], P('col', 'row'), may hold values from -6 to 6
- residual_in: float32 [1792, 1024], P('row', 'col'), may hold values from -6 to 6
- vir_energy: float32 [1792], P('row'), may hold values from 0.2 to 2
- slab_energy: float32 [128], replicated, may hold values from 0.2 to 2
- pair_energy: float32 [8], replicated, may hold values from -1 to -0.3
Outputs:
- update: float32 [1792, 1024], P('row', 'col')
All inputs are finite; a program needn't handle non-finite values.
Results may differ from a plain program's by a relative error of at most 0.0003.
Values may be sent and summed in bfloat16 or wider, within the bound.
A program may use at most 64 MiB of HBM per device.

v0:
```python
import jax
import jax.numpy as jnp
from jax import lax
from jax.sharding import PartitionSpec as P

SLAB = 128
JWIN = 8


def body(ampl, integrals, residual_in, vir_energy, slab_energy, pair_energy):
    flat_ampl = ampl.reshape(ampl.shape[0], -1)
    flat_integrals = integrals.reshape(integrals.shape[0], -1)
    left_rows, right_rows = (
        lax.all_to_all(flat_ampl, "col", split_axis=1, concat_axis=0, tiled=True),
        lax.all_to_all(flat_integrals, "col", split_axis=1, concat_axis=0, tiled=True),
    )
    contract = (((1,), (1,)), ((), ()))
    summed = lax.psum_scatter(
        lax.dot_general(right_rows, left_rows, contract, preferred_element_type=jnp.float32),
        "col",
        scatter_dimension=0,
        tiled=True,
    )
    summed = lax.psum_scatter(summed, "row", scatter_dimension=1, tiled=True)
    cycle = summed.T
    local_cols = cycle.shape[1]
    column_rank = lax.axis_index("col")
    columns = column_rank * local_cols + jnp.arange(local_cols, dtype=jnp.int32)
    slab_index = columns % SLAB
    occ_index = columns // SLAB
    slab_local = jnp.sum(
        jnp.where(
            slab_index[:, None] == jnp.arange(SLAB, dtype=jnp.int32)[None, :],
            slab_energy[None, :],
            0.0,
        ),
        axis=1,
    )
    pair_local = jnp.sum(
        jnp.where(
            occ_index[:, None] == jnp.arange(JWIN, dtype=jnp.int32)[None, :],
            pair_energy[None, :],
            0.0,
        ),
        axis=1,
    )
    denom = vir_energy[:, None] + (slab_local - pair_local)[None, :]
    return (residual_in + cycle) / denom


def solution(mesh):
    in_specs = (P("col", "row", None), P("col", "row", None), P("row", "col"), P("row"), P(), P())
    out_specs = P("row", "col")
    return jax.shard_map(body, mesh=mesh, in_specs=in_specs, out_specs=out_specs, check_vma=False)
```

profile of v0, /device:TPU:24, one launch (start us, length us, event | category | flops | bytes accessed | tf_op | source)
XLA Modules:
  0.0 457.7 jit_solution(16104272705110209047)
XLA Ops:
  6.5 5.9 %copy.11 = bf16[32,32,1792]{2,0,1:T(8,128)(2,1)} copy(bf16[32,32,1792]{2,1,0:T(8,128)(2,1)} %param.7) | data formatting | bytes 7340032 | tf_op args[1]
  12.4 11.6 %all-to-all-start = ((bf16[32,32,1792]{2,0,1:T(8,128)(2,1)}), bf16[32,32,1792]{2,0,1:T(8,128)(2,1)}, u32[]{:S(2)}, u32[]{:S(2)}) async-start(bf16[32,32,1792]{2,0,1:T(8,128)(2,1)} %copy.11), calls=%async_computation | async-start | bytes 7340032 | tf_op jit(solution)/shard_map/all_to_all | solution.py:15
  24.1 0.0 reduce-scatter.5.cloned.1.call-start
  24.1 9.1 %copy.12 = bf16[56,32,1792]{2,0,1:T(8,128)(2,1)} copy(bf16[56,32,1792]{2,1,0:T(8,128)(2,1)} %param.6) | data formatting | bytes 12845056 | tf_op args[0]
  33.2 73.6 %all-to-all-done = bf16[32,32,1792]{2,0,1:T(8,128)(2,1)} async-done(((bf16[32,32,1792]{2,0,1:T(8,128)(2,1)}), bf16[32,32,1792]{2,0,1:T(8,128)(2,1)}, u32[]{:S(2)}, u32[]{:S(2)}) %all-to-all-start) | async-done | bytes 3670048 | tf_op jit(solution)/shard_map/all_to_all | solution.py:15
  106.9 153.2 %all_to_all.32 = bf16[56,32,1792]{2,0,1:T(8,128)(2,1)S(1)} all-to-all(bf16[56,32,1792]{2,0,1:T(8,128)(2,1)} %copy.12), channel_id=1, replica_groups=mesh['row'=8,'col'=32] {'col'}, dimensions={1} | all-to-all | bytes 12845056 | tf_op jit(solution)/shard_map/all_to_all | solution.py:14
  260.1 10.4 %fusion.1 = f32[1024,1792]{1,0:T(8,128)} fusion(bf16[1024,1792]{1,0:T(8,128)(2,1)} %bitcast.1, bf16[1792,1792]{1,0:T(8,128)(2,1)S(1)} %bitcast.14), kind=kOutput, calls=%fused_computation.12 | convolution fusion | flops 6576668672 | bytes 17432576 | tf_op jit(solution)/shard_map/dot_general | solution.py:19
  270.5 0.0 copy-start.2
  270.5 0.0 copy-start.3
  270.5 0.0 copy-start
  270.5 0.0 copy-start.1
  270.5 0.0 reduce-scatter.5.cloned.1.call-update
  270.6 0.0 reduce-scatter.7.cloned.1.call-start
  270.6 136.0 %reduce-scatter.5.cloned.1.call-done = f32[32,1792]{1,0:T(8,128)} async-done(((f32[1024,1792]{1,0:T(8,128)}), f32[32,1792]{1,0:T(8,128)}) %reduce-scatter.5.cloned.1.call-update) | async-done | bytes 229392 | tf_op jit(solution)/shard_map/reduce_scatter | solution.py:18
  406.6 2.2 copy.13
  408.8 0.0 reduce-scatter.7.cloned.1.call-update
  408.8 0.0 copy-done.2
  408.9 0.2 select_reduce_fusion
  409.0 0.0 copy-done.3
  409.0 0.1 select_reduce_fusion.1
  409.1 40.1 %reduce-scatter.7.cloned.1.call-done = f32[224,32]{1,0:T(8,128)} async-done(((f32[1792,32]{1,0:T(8,128)}), f32[224,32]{1,0:T(8,128)}) %reduce-scatter.7.cloned.1.call-update) | async-done | bytes 28688
  449.2 1.0 copy.14
  450.1 0.0 copy-done
  450.2 0.0 copy-done.1
  450.2 0.7 fusion
  (2 shorter events, 0.0 us)
Async XLA Ops:
  12.4 94.4 %all-to-all-start = ((bf16[32,32,1792]{2,0,1:T(8,128)(2,1)}), bf16[32,32,1792]{2,0,1:T(8,128)(2,1)}, u32[]{:S(2)}, u32[]{:S(2)}) async-start(bf16[32,32,1792]{2,0,1:T(8,128)(2,1)} %copy.11), calls=%async_computation | async-start | bytes 7340032 | tf_op jit(solution)/shard_map/all_to_all | solution.py:15
  24.1 382.6 %reduce-scatter.5.cloned.1.call-start = ((), (), s32[]{:S(2)}) async-start(), calls=%async_computation.4 | async-start | bytes 7569408 | tf_op jit(solution)/shard_map/reduce_scatter | solution.py:18
  270.5 138.3 %copy-start.2 = (f32[128]{0:T(128)S(1)}, f32[128]{0:T(128)}, u32[]{:S(2)}) copy-start(f32[128]{0:T(128)} %param.10) | copy-start | bytes 1540
  270.5 138.5 %copy-start.3 = (f32[8]{0:T(128)S(1)}, f32[8]{0:T(128)}, u32[]{:S(2)}) copy-start(f32[8]{0:T(128)} %param.11) | copy-start | bytes 100
  270.5 179.6 %copy-start = (f32[224,32]{0,1:T(8,128)S(1)}, f32[224,32]{0,1:T(8,128)}, u32[]{:S(2)}) copy-start(f32[224,32]{0,1:T(8,128)} %param.8) | copy-start | bytes 86020
  270.5 179.6 %copy-start.1 = (f32[224]{0:T(256)S(1)}, f32[224]{0:T(256)}, u32[]{:S(2)}) copy-start(f32[224]{0:T(256)} %param.9) | copy-start | bytes 2692
  270.6 178.6 %reduce-scatter.7.cloned.1.call-start = ((), (), s32[]{:S(2)}) async-start(), calls=%async_computation.5 | async-start | bytes 1032192
Sparse Core Ops, SparseCore 0:
  270.7 135.9 reduce-scatter.4
  409.3 39.7 reduce-scatter.6
where the time goes:
time: 459 us; the launch traced here: 458 us
  waiting for transfers between devices  250 us (54%)
  blocking collectives  153 us (33%)
  local copies, waits for them, and re-layouts  18.1 us (4%)
  between operations  13.5 us (3%)
  starting transfers between devices  11.7 us (3%)
  matrix products  10.4 us (2%)
    all_to_all x1, blocking collectives, body(): lax.all_to_all(flat_ampl, 'col', split_axis=1, concat_axis=0, tiled=True)  153 us
    reduce_scatter x1, waiting for transfers between devices, body(): lax.psum_scatter(lax.dot_general(right_rows, left_rows, contract, preferr...  136 us
    all_to_all x1, waiting for transfers between devices, body(): lax.all_to_all(flat_integrals, 'col', split_axis=1, concat_axis=0, tiled=...  73.6 us
    unnamed x3, waiting for transfers between devices  40.1 us
    unnamed x12, local copies, waits for them, and re-layouts  18.1 us
    all_to_all x1, starting transfers between devices, body(): lax.all_to_all(flat_integrals, 'col', split_axis=1, concat_axis=0, tiled=...  11.6 us
    dot_general x1, matrix products, body(): lax.dot_general(right_rows, left_rows, contract, preferred_element_type=j...  10.4 us
  transfers between devices with their start and end apart: 3, of which 3 were waited for; matrix products, arithmetic and copies ran while one was open for 2% of the time, Pallas kernels for 0%

commit v1 on v0

v1 whole, which is shorter than its diff:
```python
import functools

import jax
import jax.numpy as jnp
from jax import lax
from jax.experimental import pallas as pl
from jax.experimental.pallas import tpu as pltpu
from jax.sharding import PartitionSpec as P

SLAB = 128
JWIN = 8
MESH = pl.DeviceIdType.MESH
BF = jnp.bfloat16
F32 = jnp.float32
NX, NY, NZ, NC = 4, 4, 8, 2
ZC = NZ * NC
C = 1792
A_CHUNKS = ((0, 16), (16, 16), (32, 16), (48, 8))
W_CHUNKS = ((0, 16), (16, 16))


def device(x, y, z, c):
    return ((y % 2) * NX + x, ((y // 2) * NZ + z) * NC + c)


def far_first(j):
    return jnp.where(j == NZ - 1, 0, jnp.where(j % 2 == 1, 4 - (j + 1) // 2, 4 + j // 2))


def permutation(rows):
    n = rows * 16
    out = lax.broadcasted_iota(jnp.int32, (n, n), 0)
    inp = lax.broadcasted_iota(jnp.int32, (n, n), 1)
    hit = (out // rows == inp % 16) & (out % rows == inp // 16)
    return jnp.where(hit, 1.0, 0.0).astype(BF)


def kernel(ampl, integ, out0, xbuf, x3buf, perm, perm3, sw, sa, sa3, yw, ya, ya3, rw, ra, ra3,
           half, own, r1, xr, ub, yr, zb, zr,
           load_sem, ys, yrv, zs, zrv, loc_sem, s0s, s0r, s1s, s1r, s2s, s2r, s3s, s3r):
    row = lax.axis_index("row")
    col = lax.axis_index("col")
    ylo, x = row // NX, row % NX
    yhi, z, c = col // ZC, (col // NC) % NZ, col % NC
    y = yhi * 2 + ylo
    zc = z * NC + c

    chunks = [(integ, s, n, sw.at[i], yw.at[i]) for i, (s, n) in enumerate(W_CHUNKS)]
    chunks += [(ampl, s, n, sa.at[i], ya.at[i]) for i, (s, n) in enumerate(A_CHUNKS[:-1])]
    chunks += [(ampl, *A_CHUNKS[-1], sa3, ya3)]
    nw, na = len(W_CHUNKS), len(A_CHUNKS)

    def load(i):
        src, start, rows, _, _ = chunks[i]
        dst = xbuf.at[i % 2] if rows == 16 else x3buf
        return pltpu.make_async_copy(src.at[pl.ds(start, rows)], dst, load_sem.at[i % 2])

    def relayout(i, h):
        _, _, rows, send, _ = chunks[i]

        @pl.loop(0, C // 256)
        def _(j):
            lanes = pl.ds(pl.multiple_of(j * 256, 256), 256)
            if rows == 16:
                block = xbuf[i % 2, :, 16 * h:16 * h + 16, lanes].reshape(256, 256)
                moved = jnp.dot(perm[...], block, preferred_element_type=F32)
                send[16 * h:16 * h + 16, :, lanes] = moved.astype(BF).reshape(16, 16, 256)
            else:
                block = x3buf[:, 16 * h:16 * h + 16, lanes].reshape(128, 256)
                moved = jnp.dot(perm3[...], block, preferred_element_type=F32)
                send[16 * h:16 * h + 16, :, lanes] = moved.reshape(16, rows, 256).astype(BF)

    def y_copy(i, h, zd):
        _, _, _, send, recv = chunks[i]
        return pltpu.make_async_remote_copy(
            src_ref=send.at[pl.ds(h * ZC + zd * NC, NC)],
            dst_ref=recv.at[yhi, pl.ds(zd * NC, NC)],
            send_sem=ys.at[i, h, zd],
            recv_sem=yrv.at[i, yhi, zd],
            device_id=device(x, h * 2 + 1 - ylo, z, c),
            device_id_type=MESH,
        )

    def y_arrived(i, h, zd):
        _, _, _, send, recv = chunks[i]
        return pltpu.make_async_copy(
            send.at[pl.ds(h * ZC + zd * NC, NC)], recv.at[h, pl.ds(zd * NC, NC)], yrv.at[i, h, zd])

    def slot(i, zz, cc):
        if i < nw:
            return rw.at[cc, :, zz, pl.ds(W_CHUNKS[i][0], 16)]
        xa, q = zz // 2, (zz % 2) * 2 + cc
        if i < nw + na - 1:
            return ra.at[i - nw, xa, :, q]
        return ra3.at[xa, :, q]

    def z_copy(i, zd, cd):
        recv = chunks[i][4]
        kk = zd * NC + cd
        return pltpu.make_async_remote_copy(
            src_ref=recv.at[:, kk],
            dst_ref=slot(i, z, c),
            send_sem=zs.at[i, kk],
            recv_sem=zrv.at[i, zc],
            device_id=device(x, y, zd, cd),
            device_id_type=MESH,
        )

    def z_arrived(i, zz, cc):
        recv = chunks[i][4]
        return pltpu.make_async_copy(recv.at[:, zz * NC + cc], slot(i, zz, cc), zrv.at[i, zz * NC + cc])

    def own_copy(i):
        return pltpu.make_async_copy(chunks[i][4].at[:, zc], slot(i, z, c), loc_sem.at[i])

    def prepare(i):
        load(i).wait()
        for h in range(2):
            relayout(i, h)
            if i == 0 and h == 0:
                meet()

            @pl.loop(0, NZ)
            def _(j):
                y_copy(i, h, (z + far_first(j)) % NZ).start()

        if i + 2 < nw + na:
            load(i + 2).start()

    def forward(i):
        @pl.loop(0, NZ - 1)
        def _(j):
            zd = (z + far_first(j)) % NZ
            for h in range(2):
                y_arrived(i, h, zd).wait()
            for cd in range(NC):
                z_copy(i, zd, cd).start()

        for h in range(2):
            y_arrived(i, h, z).wait()
        z_copy(i, z, 1 - c).start()
        own_copy(i).start()

    def sent(i):
        @pl.loop(0, NZ - 1)
        def _(j):
            zd = (z + far_first(j)) % NZ
            for cd in range(NC):
                z_copy(i, zd, cd).wait_send()

        z_copy(i, z, 1 - c).wait_send()

    def arrived(i):
        @pl.loop(0, NZ - 1)
        def _(j):
            zz = (z + far_first(j)) % NZ
            for cc in range(NC):
                z_arrived(i, zz, cc).wait()

        z_arrived(i, z, 1 - c).wait()
        own_copy(i).wait()

    def meet():
        barrier = pltpu.get_barrier_semaphore()
        for d in range(1, NY):
            pl.semaphore_signal(barrier, inc=1, device_id=device(x, (y + d) % NY, z, c), device_id_type=MESH)
        for d in range(1, NX):
            pl.semaphore_signal(barrier, inc=1, device_id=device((x + d) % NX, y, z, c), device_id_type=MESH)
        for d in range(1, NZ):
            for cd in range(NC):
                pl.semaphore_signal(barrier, inc=1, device_id=device(x, y, (z + d) % NZ, cd), device_id_type=MESH)
        pl.semaphore_signal(barrier, inc=1, device_id=device(x, y, z, 1 - c), device_id_type=MESH)
        pl.semaphore_wait(barrier, NY - 1 + NX - 1 + (NZ - 1) * NC + 1)

    contract = (((1,), (1,)), ((), ()))

    def multiply(m, cn, dst):
        rows = A_CHUNKS[m][1]

        @pl.loop(0, 2)
        def _(h):
            right = rw[cn, h].reshape(256, C)
            for xa in range(NX):
                if rows == 16:
                    left = ra[m, xa].reshape(128, C)
                else:
                    left = ra3[xa].astype(F32).reshape(rows * 8, C).astype(BF)
                dst[xa, :, h, :rows * 4, :] = lax.dot_general(
                    left, right, contract, preferred_element_type=F32).reshape(2, rows * 4, 256)

    def half_copy(m):
        n = A_CHUNKS[m][1] * 4
        return pltpu.make_async_remote_copy(
            src_ref=half.at[:, :, :, pl.ds(0, n)], dst_ref=r1.at[m, :, :, :, pl.ds(0, n)],
            send_sem=s0s.at[m], recv_sem=s0r.at[m],
            device_id=device(x, y, z, 1 - c), device_id_type=MESH)

    def x_copy(m, d):
        n = A_CHUNKS[m][1] * 4
        xd = (x + d) % NX
        return pltpu.make_async_remote_copy(
            src_ref=r1.at[m, xd, :, :, pl.ds(0, n)], dst_ref=xr.at[m, d - 1, :, :, pl.ds(0, n)],
            send_sem=s1s.at[m, d - 1], recv_sem=s1r.at[m, d - 1],
            device_id=device(xd, y, z, c), device_id_type=MESH)

    def yr_copy(m, d):
        n = A_CHUNKS[m][1] * 4
        yd = (y + d) % NY
        return pltpu.make_async_remote_copy(
            src_ref=ub.at[m, yd % 2, yd // 2, pl.ds(0, n)], dst_ref=yr.at[m, d - 1, pl.ds(0, n)],
            send_sem=s2s.at[m, d - 1], recv_sem=s2r.at[m, d - 1],
            device_id=device(x, yd, z, c), device_id_type=MESH)

    def zr_copy(m, d):
        zd = (z + d) % NZ
        return pltpu.make_async_remote_copy(
            src_ref=zb.at[m, zd], dst_ref=zr.at[m, d - 1],
            send_sem=s3s.at[m, d - 1], recv_sem=s3r.at[m, d - 1],
            device_id=device(x, y, zd, c), device_id_type=MESH)

    def reduce(m):
        n = A_CHUNKS[m][1] * 4
        if m > 0:
            half_copy(m - 1).wait_send()
        multiply(m, 1 - c, half)
        half_copy(m).start()
        multiply(m, c, own)
        half_copy(m).wait_recv()
        for d in (2, 1, 3, 0):
            xd = (x + d) % NX
            r1[m, xd, :, :, :n] = r1[m, xd, :, :, :n] + own[xd, :, :, :n]
            if d > 0:
                x_copy(m, d).start()
        for d in (1, 3, 2):
            x_copy(m, d).wait_recv()
        ub[m, :, :, :n] = (r1[m, x, :, :, :n] + xr[m, 0, :, :, :n]) + (xr[m, 1, :, :, :n] + xr[m, 2, :, :, :n])
        for d in (2, 1, 3):
            yr_copy(m, d).start()
        for d in (1, 3, 2):
            yr_copy(m, d).wait_recv()
        total = (ub[m, ylo, yhi, :n] + yr[m, 0, :n]) + (yr[m, 1, :n] + yr[m, 2, :n])
        if n < 64:
            total = jnp.concatenate([total, jnp.zeros_like(total)], axis=0)
        total = jnp.concatenate([total, jnp.zeros_like(total)], axis=0)
        zb[m] = total.T.reshape(NZ, 32, 128)
        for d in (4, 3, 5, 2, 6, 1, 7):
            zr_copy(m, d).start()
        for d in range(1, NZ):
            zr_copy(m, d).wait_recv()
        final = zb[m, z] + zr[m, 0]
        for d in range(2, NZ):
            final = final + zr[m, d - 1]
        out0[m] = final

    load(0).start()
    load(1).start()
    perm[...] = permutation(16)
    perm3[...] = permutation(8)

    total = nw + na
    prepare(0)
    prepare(1)
    forward(0)
    prepare(2)
    forward(1)
    prepare(3)
    sent(0)
    forward(2)
    prepare(4)
    sent(1)
    forward(3)
    prepare(5)
    arrived(0)
    arrived(1)
    arrived(2)
    sent(2)
    forward(4)
    reduce(0)
    arrived(3)
    sent(3)
    forward(5)
    reduce(1)
    arrived(4)
    reduce(2)
    arrived(5)
    reduce(3)
    sent(4)
    sent(5)
    half_copy(na - 1).wait_send()
    for m in range(na):
        for d in range(1, NX):
            x_copy(m, d).wait_send()
        for d in range(1, NY):
            yr_copy(m, d).wait_send()
        for d in range(1, NZ):
            zr_copy(m, d).wait_send()
    for i in range(total):
        for h in range(2):
            @pl.loop(0, NZ)
            def _(zd):
                y_copy(i, h, zd).wait_send()


def body(ampl, integrals, residual_in, vir_energy, slab_energy, pair_energy):
    DMA = pltpu.SemaphoreType.DMA
    nw, na = len(W_CHUNKS), len(A_CHUNKS)
    parts = pl.pallas_call(
        kernel,
        out_shape=jax.ShapeDtypeStruct((na, 32, 128), F32),
        in_specs=[pl.BlockSpec(memory_space=pl.ANY)] * 2,
        out_specs=pl.BlockSpec(memory_space=pltpu.VMEM),
        scratch_shapes=[
            pltpu.VMEM((2, 16, 32, C), BF),
            pltpu.VMEM((8, 32, C), BF),
            pltpu.VMEM((256, 256), BF),
            pltpu.VMEM((128, 128), BF),
            pltpu.VMEM((nw, 32, 16, C), BF),
            pltpu.VMEM((na - 1, 32, 16, C), BF),
            pltpu.VMEM((32, 8, C), BF),
            pltpu.VMEM((nw, 2, ZC, 16, C), BF),
            pltpu.VMEM((na - 1, 2, ZC, 16, C), BF),
            pltpu.VMEM((2, ZC, 8, C), BF),
            pltpu.VMEM((NC, 2, NZ, 32, C), BF),
            pltpu.VMEM((na - 1, NX, 2, 4, 16, C), BF),
            pltpu.VMEM((NX, 2, 4, 8, C), BF),
            pltpu.VMEM((NX, 2, 2, 64, 256), F32),
            pltpu.VMEM((NX, 2, 2, 64, 256), F32),
            pltpu.VMEM((na, NX, 2, 2, 64, 256), F32),
            pltpu.VMEM((na, NX - 1, 2, 2, 64, 256), F32),
            pltpu.VMEM((na, 2, 2, 64, 256), F32),
            pltpu.VMEM((na, NY - 1, 64, 256), F32),
            pltpu.VMEM((na, NZ, 32, 128), F32),
            pltpu.VMEM((na, NZ - 1, 32, 128), F32),
            DMA((2,)),
            DMA((nw + na, 2, NZ)), DMA((nw + na, 2, NZ)),
            DMA((nw + na, ZC)), DMA((nw + na, ZC)),
            DMA((nw + na,)),
            DMA((na,)), DMA((na,)),
            DMA((na, NX - 1)), DMA((na, NX - 1)),
            DMA((na, NY - 1)), DMA((na, NY - 1)),
            DMA((na, NZ - 1)), DMA((na, NZ - 1)),
        ],
        compiler_params=pltpu.CompilerParams(
            collective_id=0, has_side_effects=True, vmem_limit_bytes=60 * 1024 * 1024),
        cost_estimate=pl.CostEstimate(flops=2 * 1792 * 1024 * 1792, bytes_accessed=10 * 1024 * 1024, transcendentals=0),
        name="cycle",
    )(ampl, integrals)
    pieces = [parts[m, :, :4 * n].reshape(32, 4, n) for m, (_, n) in enumerate(A_CHUNKS)]
    cycle = jnp.concatenate(pieces, axis=2).reshape(32, 224).T

    local_cols = cycle.shape[1]
    columns = lax.axis_index("col") * local_cols + jnp.arange(local_cols, dtype=jnp.int32)
    slab_index = columns % SLAB
    occ_index = columns // SLAB
    slab_local = jnp.sum(
        jnp.where(slab_index[:, None] == jnp.arange(SLAB, dtype=jnp.int32)[None, :], slab_energy[None, :], 0.0), axis=1)
    pair_local = jnp.sum(
        jnp.where(occ_index[:, None] == jnp.arange(JWIN, dtype=jnp.int32)[None, :], pair_energy[None, :], 0.0), axis=1)
    denom = vir_energy[:, None] + (slab_local - pair_local)[None, :]
    return (residual_in + cycle) / denom


def solution(mesh):
    in_specs = (P("col", "row", None), P("col", "row", None), P("row", "col"), P("row"), P(), P())
    return jax.shard_map(body, mesh=mesh, in_specs=in_specs, out_specs=P("row", "col"), check_vma=False)
```

time: 459 us -> 309 us (0.67)
  Pallas kernels: 0 us -> 304 us
  waiting for transfers between devices: 250 us -> 0 us
  blocking collectives: 153 us -> 0 us
  local copies, waits for them, and re-layouts: 18.1 us -> 1.88 us
  between operations: 13.5 us -> 0.06 us
  starting transfers between devices: 11.7 us -> 0 us
  matrix products: 10.4 us -> 0 us
    pallas_call x0 -> x1, Pallas kernels: none -> 304 us  [body(): pl.pallas_call(kernel, out_shape=jax.ShapeDtypeStruct((na, 32, 128), F32)...]
    all_to_all x1 -> x0, blocking collectives: 153 us -> none  [body(): lax.all_to_all(flat_ampl, 'col', split_axis=1, concat_axis=0, tiled=True)]
    reduce_scatter x1 -> x0, waiting for transfers between devices: 136 us -> none  [body(): lax.psum_scatter(lax.dot_general(right_rows, left_rows, contract, preferr...]
    all_to_all x1 -> x0, waiting for transfers between devices: 73.6 us -> none  [body(): lax.all_to_all(flat_integrals, 'col', split_axis=1, concat_axis=0, tiled=...]
    unnamed x3 -> x0, waiting for transfers between devices: 40.1 us -> none
    unnamed x12 -> x8, local copies, waits for them, and re-layouts: 18.1 us -> 0.02 us
    all_to_all x1 -> x0, starting transfers between devices: 11.6 us -> none  [body(): lax.all_to_all(flat_integrals, 'col', split_axis=1, concat_axis=0, tiled=...]
    dot_general x1 -> x0, matrix products: 10.4 us -> none  [body(): lax.dot_general(right_rows, left_rows, contract, preferred_element_type=j...]
  transfers between devices with their start and end apart: 3 -> 0, of which waited for: 3 -> 0; matrix products, arithmetic and copies ran while one was open for 2% -> 0% of each run, Pallas kernels for 0% -> 0%
where the time goes in v1:
time: 309 us; the launch traced here: 307 us
  Pallas kernels  304 us (98%)
    pallas_call x1, Pallas kernels, body(): pl.pallas_call(kernel, out_shape=jax.ShapeDtypeStruct((na, 32, 128), F32)...  304 us

profile of v1, /device:TPU:24, one launch (start us, length us, event | category | flops | bytes accessed | tf_op | source)
XLA Modules:
  0.0 307.1 jit_solution(30761292178048171)
XLA Ops:
  0.0 0.0 copy-start.2
  0.0 0.0 copy-start.3
  0.0 0.0 copy-start
  0.0 0.0 copy-start.1
  0.0 304.2 %cycle.1 = f32[4,32,128]{2,1,0:T(8,128)} custom-call(bf16[56,32,1792]{2,1,0:T(8,128)(2,1)} %ampl.1, bf16[32,32,1792]{2,1,0:T(8,128)(2,1)} %integ.1), custom_call_target="tpu_custom_call" | custom-call | flops 6576668672 | bytes 10485760 | tf_op jit(solution)/shard_map/cycle/pallas_call | solution.py:307
  304.2 0.8 fusion.1
  305.0 0.1 copy.12
  305.0 0.1 copy.13
  305.1 0.1 copy.14
  305.2 0.7 slice.15
  305.9 0.1 copy.15
  306.0 0.1 copy.16
  306.1 0.0 copy-done.2
  306.1 0.2 select_reduce_fusion
  306.3 0.0 copy-done.3
  306.3 0.1 select_reduce_fusion.1
  306.4 0.0 copy-done
  306.4 0.0 copy-done.1
  306.4 0.7 fusion
  (3 shorter events, 0.0 us)
Async XLA Ops:
  0.0 306.1 %copy-start.2 = (f32[128]{0:T(128)S(1)}, f32[128]{0:T(128)}, u32[]{:S(2)}) copy-start(f32[128]{0:T(128)} %param.10) | copy-start | bytes 1540
  0.0 306.3 %copy-start.3 = (f32[8]{0:T(128)S(1)}, f32[8]{0:T(128)}, u32[]{:S(2)}) copy-start(f32[8]{0:T(128)} %param.11) | copy-start | bytes 100
  0.0 306.4 %copy-start = (f32[224,32]{0,1:T(8,128)S(1)}, f32[224,32]{0,1:T(8,128)}, u32[]{:S(2)}) copy-start(f32[224,32]{0,1:T(8,128)} %param.8) | copy-start | bytes 86020
  0.0 306.4 %copy-start.1 = (f32[224]{0:T(256)S(1)}, f32[224]{0:T(256)}, u32[]{:S(2)}) copy-start(f32[224]{0:T(256)} %param.9) | copy-start | bytes 2692

commit v2 on v1

--- a/solution.py
+++ b/solution.py
@@ -36,8 +36,8 @@
 
 
 def kernel(ampl, integ, out0, xbuf, x3buf, perm, perm3, sw, sa, sa3, yw, ya, ya3, rw, ra, ra3,
-           half, own, r1, xr, ub, yr, zb, zr,
-           load_sem, ys, yrv, zs, zrv, loc_sem, s0s, s0r, s1s, s1r, s2s, s2r, s3s, s3r):
+           half, own, r1, xyr, zb, zr,
+           load_sem, ys, yrv, zs, zrv, loc_sem, s0s, s0r, s1s, s1r, s3s, s3r):
     row = lax.axis_index("row")
     col = lax.axis_index("col")
     ylo, x = row // NX, row % NX
@@ -162,15 +162,14 @@
 
     def meet():
         barrier = pltpu.get_barrier_semaphore()
-        for d in range(1, NY):
-            pl.semaphore_signal(barrier, inc=1, device_id=device(x, (y + d) % NY, z, c), device_id_type=MESH)
-        for d in range(1, NX):
-            pl.semaphore_signal(barrier, inc=1, device_id=device((x + d) % NX, y, z, c), device_id_type=MESH)
+        for off in range(1, NX * NY):
+            peer = device((x + off // NY) % NX, (y + off % NY) % NY, z, c)
+            pl.semaphore_signal(barrier, inc=1, device_id=peer, device_id_type=MESH)
         for d in range(1, NZ):
             for cd in range(NC):
                 pl.semaphore_signal(barrier, inc=1, device_id=device(x, y, (z + d) % NZ, cd), device_id_type=MESH)
         pl.semaphore_signal(barrier, inc=1, device_id=device(x, y, z, 1 - c), device_id_type=MESH)
-        pl.semaphore_wait(barrier, NY - 1 + NX - 1 + (NZ - 1) * NC + 1)
+        pl.semaphore_wait(barrier, NX * NY - 1 + (NZ - 1) * NC + 1)
 
     contract = (((1,), (1,)), ((), ()))
 
@@ -195,30 +194,23 @@
             send_sem=s0s.at[m], recv_sem=s0r.at[m],
             device_id=device(x, y, z, 1 - c), device_id_type=MESH)
 
-    def x_copy(m, d):
+    def xy_copy(m, off):
         n = A_CHUNKS[m][1] * 4
-        xd = (x + d) % NX
-        return pltpu.make_async_remote_copy(
-            src_ref=r1.at[m, xd, :, :, pl.ds(0, n)], dst_ref=xr.at[m, d - 1, :, :, pl.ds(0, n)],
-            send_sem=s1s.at[m, d - 1], recv_sem=s1r.at[m, d - 1],
-            device_id=device(xd, y, z, c), device_id_type=MESH)
-
-    def yr_copy(m, d):
-        n = A_CHUNKS[m][1] * 4
-        yd = (y + d) % NY
-        return pltpu.make_async_remote_copy(
-            src_ref=ub.at[m, yd % 2, yd // 2, pl.ds(0, n)], dst_ref=yr.at[m, d - 1, pl.ds(0, n)],
-            send_sem=s2s.at[m, d - 1], recv_sem=s2r.at[m, d - 1],
-            device_id=device(x, yd, z, c), device_id_type=MESH)
-
-    def zr_copy(m, d):
-        zd = (z + d) % NZ
-        return pltpu.make_async_remote_copy(
-            src_ref=zb.at[m, zd], dst_ref=zr.at[m, d - 1],
-            send_sem=s3s.at[m, d - 1], recv_sem=s3r.at[m, d - 1],
+        xd, yd = (x + off // NY) % NX, (y + off % NY) % NY
+        return pltpu.make_async_remote_copy(
+            src_ref=r1.at[m, xd, yd % 2, yd // 2, pl.ds(0, n)], dst_ref=xyr.at[m, off - 1, pl.ds(0, n)],
+            send_sem=s1s.at[m, off - 1], recv_sem=s1r.at[m, off - 1],
+            device_id=device(xd, yd, z, c), device_id_type=MESH)
+
+    def zr_copy(g, j):
+        off = far_first(j)
+        zd = (z + off) % NZ
+        return pltpu.make_async_remote_copy(
+            src_ref=zb.at[g, zd], dst_ref=zr.at[g, off - 1],
+            send_sem=s3s.at[g, off - 1], recv_sem=s3r.at[g, off - 1],
             device_id=device(x, y, zd, c), device_id_type=MESH)
 
-    def reduce(m):
+    def pair_stage(m):
         n = A_CHUNKS[m][1] * 4
         if m > 0:
             half_copy(m - 1).wait_send()
@@ -229,35 +221,48 @@
         for d in (2, 1, 3, 0):
             xd = (x + d) % NX
             r1[m, xd, :, :, :n] = r1[m, xd, :, :, :n] + own[xd, :, :, :n]
-            if d > 0:
-                x_copy(m, d).start()
-        for d in (1, 3, 2):
-            x_copy(m, d).wait_recv()
-        ub[m, :, :, :n] = (r1[m, x, :, :, :n] + xr[m, 0, :, :, :n]) + (xr[m, 1, :, :, :n] + xr[m, 2, :, :, :n])
-        for d in (2, 1, 3):
-            yr_copy(m, d).start()
-        for d in (1, 3, 2):
-            yr_copy(m, d).wait_recv()
-        total = (ub[m, ylo, yhi, :n] + yr[m, 0, :n]) + (yr[m, 1, :n] + yr[m, 2, :n])
+
+            @pl.loop(0 if d > 0 else 1, NY)
+            def _(j):
+                xy_copy(m, d * NY + j).start()
+
+    def gathered(m):
+        n = A_CHUNKS[m][1] * 4
+
+        @pl.loop(1, NX * NY)
+        def _(off):
+            xy_copy(m, off).wait_recv()
+
+        total = r1[m, x, ylo, yhi, :n]
+        for off in range(1, NX * NY):
+            total = total + xyr[m, off - 1, :n]
         if n < 64:
             total = jnp.concatenate([total, jnp.zeros_like(total)], axis=0)
-        total = jnp.concatenate([total, jnp.zeros_like(total)], axis=0)
-        zb[m] = total.T.reshape(NZ, 32, 128)
-        for d in (4, 3, 5, 2, 6, 1, 7):
-            zr_copy(m, d).start()
+        return total
+
+    def plane_stage(g):
+        both = jnp.concatenate([gathered(2 * g), gathered(2 * g + 1)], axis=0)
+        zb[g] = both.T.reshape(NZ, 32, 128)
+
+        @pl.loop(0, NZ - 1)
+        def _(j):
+            zr_copy(g, j).start()
+
+    def last_stage(g):
+        @pl.loop(0, NZ - 1)
+        def _(j):
+            zr_copy(g, j).wait_recv()
+
+        final = zb[g, z]
         for d in range(1, NZ):
-            zr_copy(m, d).wait_recv()
-        final = zb[m, z] + zr[m, 0]
-        for d in range(2, NZ):
-            final = final + zr[m, d - 1]
-        out0[m] = final
+            final = final + zr[g, d - 1]
+        out0[g] = final
 
     load(0).start()
     load(1).start()
     perm[...] = permutation(16)
     perm3[...] = permutation(8)
 
-    total = nw + na
     prepare(0)
     prepare(1)
     forward(0)
@@ -275,26 +280,32 @@
     arrived(2)
     sent(2)
     forward(4)
-    reduce(0)
+    pair_stage(0)
     arrived(3)
     sent(3)
     forward(5)
-    reduce(1)
+    pair_stage(1)
+    plane_stage(0)
     arrived(4)
-    reduce(2)
+    pair_stage(2)
     arrived(5)
-    reduce(3)
+    pair_stage(3)
+    plane_stage(1)
+    last_stage(0)
+    last_stage(1)
+
     sent(4)
     sent(5)
     half_copy(na - 1).wait_send()
     for m in range(na):
-        for d in range(1, NX):
-            x_copy(m, d).wait_send()
-        for d in range(1, NY):
-            yr_copy(m, d).wait_send()
-        for d in range(1, NZ):
-            zr_copy(m, d).wait_send()
-    for i in range(total):
+        @pl.loop(1, NX * NY)
+        def _(off):
+            xy_copy(m, off).wait_send()
+    for g in range(na // 2):
+        @pl.loop(0, NZ - 1)
+        def _(j):
+            zr_copy(g, j).wait_send()
+    for i in range(nw + na):
         for h in range(2):
             @pl.loop(0, NZ)
             def _(zd):
@@ -306,7 +317,7 @@
     nw, na = len(W_CHUNKS), len(A_CHUNKS)
     parts = pl.pallas_call(
         kernel,
-        out_shape=jax.ShapeDtypeStruct((na, 32, 128), F32),
+        out_shape=jax.ShapeDtypeStruct((na // 2, 32, 128), F32),
         in_specs=[pl.BlockSpec(memory_space=pl.ANY)] * 2,
         out_specs=pl.BlockSpec(memory_space=pltpu.VMEM),
         scratch_shapes=[
@@ -326,26 +337,24 @@
             pltpu.VMEM((NX, 2, 2, 64, 256), F32),
             pltpu.VMEM((NX, 2, 2, 64, 256), F32),
             pltpu.VMEM((na, NX, 2, 2, 64, 256), F32),
-            pltpu.VMEM((na, NX - 1, 2, 2, 64, 256), F32),
-            pltpu.VMEM((na, 2, 2, 64, 256), F32),
-            pltpu.VMEM((na, NY - 1, 64, 256), F32),
-            pltpu.VMEM((na, NZ, 32, 128), F32),
-            pltpu.VMEM((na, NZ - 1, 32, 128), F32),
+            pltpu.VMEM((na, NX * NY - 1, 64, 256), F32),
+            pltpu.VMEM((na // 2, NZ, 32, 128), F32),
+            pltpu.VMEM((na // 2, NZ - 1, 32, 128), F32),
             DMA((2,)),
             DMA((nw + na, 2, NZ)), DMA((nw + na, 2, NZ)),
             DMA((nw + na, ZC)), DMA((nw + na, ZC)),
             DMA((nw + na,)),
             DMA((na,)), DMA((na,)),
-            DMA((na, NX - 1)), DMA((na, NX - 1)),
-            DMA((na, NY - 1)), DMA((na, NY - 1)),
-            DMA((na, NZ - 1)), DMA((na, NZ - 1)),
+            DMA((na, NX * NY - 1)), DMA((na, NX * NY - 1)),
+            DMA((na // 2, NZ - 1)), DMA((na // 2, NZ - 1)),
         ],
         compiler_params=pltpu.CompilerParams(
             collective_id=0, has_side_effects=True, vmem_limit_bytes=60 * 1024 * 1024),
         cost_estimate=pl.CostEstimate(flops=2 * 1792 * 1024 * 1792, bytes_accessed=10 * 1024 * 1024, transcendentals=0),
         name="cycle",
     )(ampl, integrals)
-    pieces = [parts[m, :, :4 * n].reshape(32, 4, n) for m, (_, n) in enumerate(A_CHUNKS)]
+    pieces = [
+        parts[m // 2, :, m % 2 * 64:m % 2 * 64 + 4 * n].reshape(32, 4, n) for m, (_, n) in enumerate(A_CHUNKS)]
     cycle = jnp.concatenate(pieces, axis=2).reshape(32, 224).T
 
     local_cols = cycle.shape[1]

time: 309 us -> 268 us (0.87)
  Pallas kernels: 304 us -> 263 us
    pallas_call x1, Pallas kernels: 304 us -> 263 us  [body(): pl.pallas_call(kernel, out_shape=jax.ShapeDtypeStruct((na // 2, 32, 128),...]
where the time goes in v2:
time: 268 us; the launch traced here: 266 us
  Pallas kernels  263 us (98%)
    pallas_call x1, Pallas kernels, body(): pl.pallas_call(kernel, out_shape=jax.ShapeDtypeStruct((na // 2, 32, 128),...  263 us

profile of v2, /device:TPU:24, one launch (start us, length us, event | category | flops | bytes accessed | tf_op | source)
XLA Modules:
  0.0 265.7 jit_solution(5209034643737342226)
XLA Ops:
  0.0 0.0 copy-start.2
  0.0 0.0 copy-start.3
  0.0 0.0 copy-start
  0.0 0.0 copy-start.1
  0.0 262.6 %cycle.1 = f32[2,32,128]{2,1,0:T(8,128)} custom-call(bf16[56,32,1792]{2,1,0:T(8,128)(2,1)} %ampl.1, bf16[32,32,1792]{2,1,0:T(8,128)(2,1)} %integ.1), custom_call_target="tpu_custom_call" | custom-call | flops 6576668672 | bytes 10485760 | tf_op jit(solution)/shard_map/cycle/pallas_call | solution.py:318
  262.6 0.9 fusion.1
  263.5 0.1 copy.12
  263.6 0.1 copy.13
  263.6 0.1 copy.14
  263.7 0.8 slice.15
  264.5 0.1 copy.15
  264.6 0.1 copy.16
  264.7 0.0 copy-done.2
  264.7 0.2 select_reduce_fusion
  264.9 0.0 copy-done.3
  264.9 0.1 select_reduce_fusion.1
  265.0 0.0 copy-done
  265.0 0.0 copy-done.1
  265.0 0.7 fusion
  (3 shorter events, 0.0 us)
Async XLA Ops:
  0.0 264.7 %copy-start.2 = (f32[128]{0:T(128)S(1)}, f32[128]{0:T(128)}, u32[]{:S(2)}) copy-start(f32[128]{0:T(128)} %param.10) | copy-start | bytes 1540
  0.0 264.9 %copy-start.3 = (f32[8]{0:T(128)S(1)}, f32[8]{0:T(128)}, u32[]{:S(2)}) copy-start(f32[8]{0:T(128)} %param.11) | copy-start | bytes 100
  0.0 265.0 %copy-start = (f32[224,32]{0,1:T(8,128)S(1)}, f32[224,32]{0,1:T(8,128)}, u32[]{:S(2)}) copy-start(f32[224,32]{0,1:T(8,128)} %param.8) | copy-start | bytes 86020
  0.0 265.0 %copy-start.1 = (f32[224]{0:T(256)S(1)}, f32[224]{0:T(256)}, u32[]{:S(2)}) copy-start(f32[224]{0:T(256)} %param.9) | copy-start | bytes 2692

commit v3 on v2

--- a/solution.py
+++ b/solution.py
@@ -27,6 +27,10 @@
     return jnp.where(j == NZ - 1, 0, jnp.where(j % 2 == 1, 4 - (j + 1) // 2, 4 + j // 2))
 
 
+def need_order(t):
+    return jnp.where(t % 2 == 0, 3 - t // 2, 4 + t // 2)
+
+
 def permutation(rows):
     n = rows * 16
     out = lax.broadcasted_iota(jnp.int32, (n, n), 0)
@@ -37,7 +41,7 @@
 
 def kernel(ampl, integ, out0, xbuf, x3buf, perm, perm3, sw, sa, sa3, yw, ya, ya3, rw, ra, ra3,
            half, own, r1, xyr, zb, zr,
-           load_sem, ys, yrv, zs, zrv, loc_sem, s0s, s0r, s1s, s1r, s3s, s3r):
+           load_sem, ys, yrv, zs, zrv, ws, wrv, loc_sem, s0s, s0r, s1s, s1r, s3s, s3r):
     row = lax.axis_index("row")
     col = lax.axis_index("col")
     ylo, x = row // NX, row % NX
@@ -86,32 +90,48 @@
         return pltpu.make_async_copy(
             send.at[pl.ds(h * ZC + zd * NC, NC)], recv.at[h, pl.ds(zd * NC, NC)], yrv.at[i, h, zd])
 
-    def slot(i, zz, cc):
+    def source(role, j):
+        return (z - j if role == 0 else z + j) % NZ
+
+    def slot(i, role, j, zz, cc):
         if i < nw:
-            return rw.at[cc, :, zz, pl.ds(W_CHUNKS[i][0], 16)]
-        xa, q = zz // 2, (zz % 2) * 2 + cc
+            return rw.at[role, cc, :, zz, pl.ds(W_CHUNKS[i][0], 16)]
         if i < nw + na - 1:
-            return ra.at[i - nw, xa, :, q]
-        return ra3.at[xa, :, q]
-
-    def z_copy(i, zd, cd):
-        recv = chunks[i][4]
-        kk = zd * NC + cd
-        return pltpu.make_async_remote_copy(
-            src_ref=recv.at[:, kk],
-            dst_ref=slot(i, z, c),
-            send_sem=zs.at[i, kk],
-            recv_sem=zrv.at[i, zc],
+            return ra.at[i - nw, role, j, :, cc]
+        return ra3.at[role, j, :, cc]
+
+    def z_copy(i, role, j, cd):
+        zd = (z + j if role == 0 else z - j) % NZ
+        kk = (zd - role) % NZ * NC + cd
+        return pltpu.make_async_remote_copy(
+            src_ref=chunks[i][4].at[:, kk],
+            dst_ref=slot(i, role, j, z, c),
+            send_sem=zs.at[i, role, j, cd],
+            recv_sem=zrv.at[i, role, j, c],
             device_id=device(x, y, zd, cd),
             device_id_type=MESH,
         )
 
-    def z_arrived(i, zz, cc):
-        recv = chunks[i][4]
-        return pltpu.make_async_copy(recv.at[:, zz * NC + cc], slot(i, zz, cc), zrv.at[i, zz * NC + cc])
-
-    def own_copy(i):
-        return pltpu.make_async_copy(chunks[i][4].at[:, zc], slot(i, z, c), loc_sem.at[i])
+    def z_arrived(i, role, j, cc):
+        dst = slot(i, role, j, source(role, j), cc)
+        return pltpu.make_async_copy(chunks[i][4].at[:, cc], dst, zrv.at[i, role, j, cc])
+
+    def own_copy(i, role):
+        kk = (z - role) % NZ * NC + c
+        return pltpu.make_async_copy(chunks[i][4].at[:, kk], slot(i, role, 0, z, c), loc_sem.at[i, role])
+
+    def pass_copy(i, role, j, cc):
+        ref = slot(i, role, j, source(role, j), cc)
+        dst = slot(i, 1 - role, j, source(role, j), cc)
+        return pltpu.make_async_remote_copy(
+            src_ref=ref, dst_ref=dst,
+            send_sem=ws.at[i, role, j, cc], recv_sem=wrv.at[i, 1 - role, j, cc],
+            device_id=device(x, y, (z + 1 - 2 * role) % NZ, c), device_id_type=MESH)
+
+    def passed(i, role, j, cc):
+        zz = (z - 1 - j if role == 1 else z + 1 + j) % NZ
+        dst = slot(i, role, j, zz, cc)
+        return pltpu.make_async_copy(chunks[i][4].at[:, cc], dst, wrv.at[i, role, j, cc])
 
     def prepare(i):
         load(i).wait()
@@ -122,43 +142,60 @@
 
             @pl.loop(0, NZ)
             def _(j):
-                y_copy(i, h, (z + far_first(j)) % NZ).start()
+                y_copy(i, h, (z + need_order(j)) % NZ).start()
 
         if i + 2 < nw + na:
             load(i + 2).start()
 
     def forward(i):
-        @pl.loop(0, NZ - 1)
-        def _(j):
-            zd = (z + far_first(j)) % NZ
+        @pl.loop(0, 3)
+        def _(t):
+            j = 3 - t
+            for role in range(2):
+                kz = (z + j if role == 0 else z - j - 1) % NZ
+                for h in range(2):
+                    y_arrived(i, h, kz).wait()
+                for cd in range(NC):
+                    z_copy(i, role, j, cd).start()
+
+        for role in range(2):
             for h in range(2):
-                y_arrived(i, h, zd).wait()
-            for cd in range(NC):
-                z_copy(i, zd, cd).start()
-
-        for h in range(2):
-            y_arrived(i, h, z).wait()
-        z_copy(i, z, 1 - c).start()
-        own_copy(i).start()
+                y_arrived(i, h, (z - role) % NZ).wait()
+            z_copy(i, role, 0, 1 - c).start()
+            own_copy(i, role).start()
 
     def sent(i):
-        @pl.loop(0, NZ - 1)
-        def _(j):
-            zd = (z + far_first(j)) % NZ
-            for cd in range(NC):
-                z_copy(i, zd, cd).wait_send()
-
-        z_copy(i, z, 1 - c).wait_send()
-
-    def arrived(i):
-        @pl.loop(0, NZ - 1)
-        def _(j):
-            zz = (z + far_first(j)) % NZ
-            for cc in range(NC):
-                z_arrived(i, zz, cc).wait()
-
-        z_arrived(i, z, 1 - c).wait()
-        own_copy(i).wait()
+        @pl.loop(1, 4)
+        def _(j):
+            for role in range(2):
+                for cd in range(NC):
+                    z_copy(i, role, j, cd).wait_send()
+
+        for role in range(2):
+            z_copy(i, role, 0, 1 - c).wait_send()
+
+    def arrived(i, then=None):
+        for role in range(2):
+            z_arrived(i, role, 0, 1 - c).wait()
+            own_copy(i, role).wait()
+            if then is not None:
+                for cc in range(NC):
+                    then(i, role, 0, cc).start()
+
+        @pl.loop(1, 4)
+        def _(j):
+            for role in range(2):
+                for cc in range(NC):
+                    z_arrived(i, role, j, cc).wait()
+                    if then is not None:
+                        then(i, role, j, cc).start()
+
+    def complete(i):
+        @pl.loop(0, 4)
+        def _(j):
+            for role in range(2):
+                for cc in range(NC):
+                    passed(i, role, j, cc).wait()
 
     def meet():
         barrier = pltpu.get_barrier_semaphore()
@@ -175,30 +212,39 @@
 
     def multiply(m, cn, dst):
         rows = A_CHUNKS[m][1]
+        n = rows * 2
 
         @pl.loop(0, 2)
         def _(h):
-            right = rw[cn, h].reshape(256, C)
-            for xa in range(NX):
+            parts = []
+            for role in range(2):
                 if rows == 16:
-                    left = ra[m, xa].reshape(128, C)
+                    left = ra[m, role].reshape(256, C)
                 else:
-                    left = ra3[xa].astype(F32).reshape(rows * 8, C).astype(BF)
-                dst[xa, :, h, :rows * 4, :] = lax.dot_general(
-                    left, right, contract, preferred_element_type=F32).reshape(2, rows * 4, 256)
+                    left = ra3[role].astype(F32).reshape(rows * 16, C).astype(BF)
+                part = lax.dot_general(
+                    left, rw[role, cn, h].reshape(256, C), contract, preferred_element_type=F32)
+                parts.append(part.reshape(4, 2, n, 256))
+            for role in range(2):
+                for j in range(1, 4):
+                    zz = source(role, j)
+                    dst[zz // 2, :, h, zz % 2, :n, :] = parts[role][j]
+            dst[z // 2, :, h, z % 2, :n, :] = parts[0][0] + parts[1][0]
+            zz = (z + 4) % NZ
+            dst[zz // 2, :, h, zz % 2, :n, :] = jnp.zeros((2, n, 256), F32)
 
     def half_copy(m):
-        n = A_CHUNKS[m][1] * 4
-        return pltpu.make_async_remote_copy(
-            src_ref=half.at[:, :, :, pl.ds(0, n)], dst_ref=r1.at[m, :, :, :, pl.ds(0, n)],
+        n = A_CHUNKS[m][1] * 2
+        return pltpu.make_async_remote_copy(
+            src_ref=half.at[:, :, :, :, pl.ds(0, n)], dst_ref=r1.at[m, :, :, :, :, pl.ds(0, n)],
             send_sem=s0s.at[m], recv_sem=s0r.at[m],
             device_id=device(x, y, z, 1 - c), device_id_type=MESH)
 
     def xy_copy(m, off):
-        n = A_CHUNKS[m][1] * 4
+        n = A_CHUNKS[m][1] * 2
         xd, yd = (x + off // NY) % NX, (y + off % NY) % NY
         return pltpu.make_async_remote_copy(
-            src_ref=r1.at[m, xd, yd % 2, yd // 2, pl.ds(0, n)], dst_ref=xyr.at[m, off - 1, pl.ds(0, n)],
+            src_ref=r1.at[m, xd, yd % 2, yd // 2, :, pl.ds(0, n)], dst_ref=xyr.at[m, off - 1, :, pl.ds(0, n)],
             send_sem=s1s.at[m, off - 1], recv_sem=s1r.at[m, off - 1],
             device_id=device(xd, yd, z, c), device_id_type=MESH)
 
@@ -211,7 +257,7 @@
             device_id=device(x, y, zd, c), device_id_type=MESH)
 
     def pair_stage(m):
-        n = A_CHUNKS[m][1] * 4
+        n = A_CHUNKS[m][1] * 2
         if m > 0:
             half_copy(m - 1).wait_send()
         multiply(m, 1 - c, half)
@@ -220,23 +266,24 @@
         half_copy(m).wait_recv()
         for d in (2, 1, 3, 0):
             xd = (x + d) % NX
-            r1[m, xd, :, :, :n] = r1[m, xd, :, :, :n] + own[xd, :, :, :n]
+            r1[m, xd, :, :, :, :n] = r1[m, xd, :, :, :, :n] + own[xd, :, :, :, :n]
 
             @pl.loop(0 if d > 0 else 1, NY)
             def _(j):
                 xy_copy(m, d * NY + j).start()
 
     def gathered(m):
-        n = A_CHUNKS[m][1] * 4
+        n = A_CHUNKS[m][1] * 2
 
         @pl.loop(1, NX * NY)
         def _(off):
             xy_copy(m, off).wait_recv()
 
-        total = r1[m, x, ylo, yhi, :n]
+        total = r1[m, x, ylo, yhi, :, :n]
         for off in range(1, NX * NY):
-            total = total + xyr[m, off - 1, :n]
-        if n < 64:
+            total = total + xyr[m, off - 1, :, :n]
+        total = total.reshape(2 * n, 256)
+        if n < 32:
             total = jnp.concatenate([total, jnp.zeros_like(total)], axis=0)
         return total
 
@@ -269,14 +316,16 @@
     prepare(2)
     forward(1)
     prepare(3)
+    arrived(0, pass_copy)
     sent(0)
     forward(2)
     prepare(4)
+    arrived(1, pass_copy)
     sent(1)
     forward(3)
     prepare(5)
-    arrived(0)
-    arrived(1)
+    complete(0)
+    complete(1)
     arrived(2)
     sent(2)
     forward(4)
@@ -305,6 +354,12 @@
         @pl.loop(0, NZ - 1)
         def _(j):
             zr_copy(g, j).wait_send()
+    for i in range(nw):
+        @pl.loop(0, 4)
+        def _(j):
+            for role in range(2):
+                for cc in range(NC):
+                    pass_copy(i, role, j, cc).wait_send()
     for i in range(nw + na):
         for h in range(2):
             @pl.loop(0, NZ)
@@ -331,19 +386,20 @@
             pltpu.VMEM((nw, 2, ZC, 16, C), BF),
             pltpu.VMEM((na - 1, 2, ZC, 16, C), BF),
             pltpu.VMEM((2, ZC, 8, C), BF),
-            pltpu.VMEM((NC, 2, NZ, 32, C), BF),
-            pltpu.VMEM((na - 1, NX, 2, 4, 16, C), BF),
-            pltpu.VMEM((NX, 2, 4, 8, C), BF),
-            pltpu.VMEM((NX, 2, 2, 64, 256), F32),
-            pltpu.VMEM((NX, 2, 2, 64, 256), F32),
-            pltpu.VMEM((na, NX, 2, 2, 64, 256), F32),
-            pltpu.VMEM((na, NX * NY - 1, 64, 256), F32),
+            pltpu.VMEM((2, NC, 2, NZ, 32, C), BF),
+            pltpu.VMEM((na - 1, 2, 4, 2, NC, 16, C), BF),
+            pltpu.VMEM((2, 4, 2, NC, 8, C), BF),
+            pltpu.VMEM((NX, 2, 2, 2, 32, 256), F32),
+            pltpu.VMEM((NX, 2, 2, 2, 32, 256), F32),
+            pltpu.VMEM((na, NX, 2, 2, 2, 32, 256), F32),
+            pltpu.VMEM((na, NX * NY - 1, 2, 32, 256), F32),
             pltpu.VMEM((na // 2, NZ, 32, 128), F32),
             pltpu.VMEM((na // 2, NZ - 1, 32, 128), F32),
             DMA((2,)),
             DMA((nw + na, 2, NZ)), DMA((nw + na, 2, NZ)),
-            DMA((nw + na, ZC)), DMA((nw + na, ZC)),
-            DMA((nw + na,)),
+            DMA((nw + na, 2, 4, NC)), DMA((nw + na, 2, 4, NC)),
+            DMA((nw, 2, 4, NC)), DMA((nw, 2, 4, NC)),
+            DMA((nw + na, 2)),
             DMA((na,)), DMA((na,)),
             DMA((na, NX * NY - 1)), DMA((na, NX * NY - 1)),
             DMA((na // 2, NZ - 1)), DMA((na // 2, NZ - 1)),

time: 268 us -> 254 us (0.948)
  Pallas kernels: 263 us -> 248 us
    pallas_call x1, Pallas kernels: 263 us -> 248 us  [body(): pl.pallas_call(kernel, out_shape=jax.ShapeDtypeStruct((na // 2, 32, 128),...]
where the time goes in v3:
time: 254 us; the launch traced here: 252 us
  Pallas kernels  248 us (98%)
    pallas_call x1, Pallas kernels, body(): pl.pallas_call(kernel, out_shape=jax.ShapeDtypeStruct((na // 2, 32, 128),...  248 us

profile of v3, /device:TPU:24, one launch (start us, length us, event | category | flops | bytes accessed | tf_op | source)
XLA Modules:
  0.0 251.5 jit_solution(8925050929176442671)
XLA Ops:
  0.0 0.0 copy-start.2
  0.0 0.0 copy-start.3
  0.0 0.0 copy-start
  0.0 0.0 copy-start.1
  0.0 248.4 %cycle.1 = f32[2,32,128]{2,1,0:T(8,128)} custom-call(bf16[56,32,1792]{2,1,0:T(8,128)(2,1)} %ampl.1, bf16[32,32,1792]{2,1,0:T(8,128)(2,1)} %integ.1), custom_call_target="tpu_custom_call" | custom-call | flops 6576668672 | bytes 10485760 | tf_op jit(solution)/shard_map/cycle/pallas_call | solution.py:373
  248.4 0.9 fusion.1
  249.3 0.1 copy.12
  249.4 0.1 copy.13
  249.5 0.1 copy.14
  249.6 0.8 slice.15
  250.4 0.1 copy.15
  250.4 0.1 copy.16
  250.5 0.0 copy-done.2
  250.6 0.2 select_reduce_fusion
  250.7 0.0 copy-done.3
  250.7 0.1 select_reduce_fusion.1
  250.8 0.0 copy-done
  250.8 0.0 copy-done.1
  250.8 0.7 fusion
  (3 shorter events, 0.0 us)
Async XLA Ops:
  0.0 250.5 %copy-start.2 = (f32[128]{0:T(128)S(1)}, f32[128]{0:T(128)}, u32[]{:S(2)}) copy-start(f32[128]{0:T(128)} %param.10) | copy-start | bytes 1540
  0.0 250.7 %copy-start.3 = (f32[8]{0:T(128)S(1)}, f32[8]{0:T(128)}, u32[]{:S(2)}) copy-start(f32[8]{0:T(128)} %param.11) | copy-start | bytes 100
  0.0 250.8 %copy-start = (f32[224,32]{0,1:T(8,128)S(1)}, f32[224,32]{0,1:T(8,128)}, u32[]{:S(2)}) copy-start(f32[224,32]{0,1:T(8,128)} %param.8) | copy-start | bytes 86020
  0.0 250.8 %copy-start.1 = (f32[224]{0:T(256)S(1)}, f32[224]{0:T(256)}, u32[]{:S(2)}) copy-start(f32[224]{0:T(256)} %param.9) | copy-start | bytes 2692

commit v4 on v3

--- a/solution.py
+++ b/solution.py
@@ -33,15 +33,16 @@
 
 def permutation(rows):
     n = rows * 16
+    bits = rows.bit_length() - 1
     out = lax.broadcasted_iota(jnp.int32, (n, n), 0)
     inp = lax.broadcasted_iota(jnp.int32, (n, n), 1)
-    hit = (out // rows == inp % 16) & (out % rows == inp // 16)
+    hit = ((out >> bits) == (inp & 15)) & ((out & (rows - 1)) == (inp >> 4))
     return jnp.where(hit, 1.0, 0.0).astype(BF)
 
 
-def kernel(ampl, integ, out0, xbuf, x3buf, perm, perm3, sw, sa, sa3, yw, ya, ya3, rw, ra, ra3,
-           half, own, r1, xyr, zb, zr,
-           load_sem, ys, yrv, zs, zrv, ws, wrv, loc_sem, s0s, s0r, s1s, s1r, s3s, s3r):
+def kernel(ampl, integ, residual, vir, slab, pair, out, xbuf, x3buf, perm, perm3, sw, sa, sa3, yw, ya, ya3, rw, ra, ra3,
+           half, own, r1, xyr, zb, zr, res_v, vir_v, slab_v, pair_v,
+           load_sem, first_sem, small_sem, ys, yrv, zs, zrv, ws, wrv, loc_sem, s0s, s0r, s1s, s1r, s3s, s3r):
     row = lax.axis_index("row")
     col = lax.axis_index("col")
     ylo, x = row // NX, row % NX
@@ -58,6 +59,10 @@
         src, start, rows, _, _ = chunks[i]
         dst = xbuf.at[i % 2] if rows == 16 else x3buf
         return pltpu.make_async_copy(src.at[pl.ds(start, rows)], dst, load_sem.at[i % 2])
+
+    def first_load(h):
+        ks = pl.ds(16 * h, 16)
+        return pltpu.make_async_copy(integ.at[pl.ds(0, 16), ks], xbuf.at[0, :, ks], first_sem.at[h])
 
     def relayout(i, h):
         _, _, rows, send, _ = chunks[i]
@@ -134,11 +139,14 @@
         return pltpu.make_async_copy(chunks[i][4].at[:, cc], dst, wrv.at[i, role, j, cc])
 
     def prepare(i):
-        load(i).wait()
+        if i > 0:
+            load(i).wait()
         for h in range(2):
+            if i == 0:
+                first_load(h).wait()
             relayout(i, h)
             if i == 0 and h == 0:
-                meet()
+                pl.semaphore_wait(barrier, NX * NY - 1 + (NZ - 1) * NC + 1)
 
             @pl.loop(0, NZ)
             def _(j):
@@ -197,47 +205,34 @@
                 for cc in range(NC):
                     passed(i, role, j, cc).wait()
 
-    def meet():
-        barrier = pltpu.get_barrier_semaphore()
-        for off in range(1, NX * NY):
-            peer = device((x + off // NY) % NX, (y + off % NY) % NY, z, c)
-            pl.semaphore_signal(barrier, inc=1, device_id=peer, device_id_type=MESH)
-        for d in range(1, NZ):
-            for cd in range(NC):
-                pl.semaphore_signal(barrier, inc=1, device_id=device(x, y, (z + d) % NZ, cd), device_id_type=MESH)
-        pl.semaphore_signal(barrier, inc=1, device_id=device(x, y, z, 1 - c), device_id_type=MESH)
-        pl.semaphore_wait(barrier, NX * NY - 1 + (NZ - 1) * NC + 1)
-
     contract = (((1,), (1,)), ((), ()))
 
-    def multiply(m, cn, dst):
+    def multiply(m, cn, dst, h):
         rows = A_CHUNKS[m][1]
         n = rows * 2
 
-        @pl.loop(0, 2)
-        def _(h):
-            parts = []
-            for role in range(2):
-                if rows == 16:
-                    left = ra[m, role].reshape(256, C)
-                else:
-                    left = ra3[role].astype(F32).reshape(rows * 16, C).astype(BF)
-                part = lax.dot_general(
-                    left, rw[role, cn, h].reshape(256, C), contract, preferred_element_type=F32)
-                parts.append(part.reshape(4, 2, n, 256))
-            for role in range(2):
-                for j in range(1, 4):
-                    zz = source(role, j)
-                    dst[zz // 2, :, h, zz % 2, :n, :] = parts[role][j]
-            dst[z // 2, :, h, z % 2, :n, :] = parts[0][0] + parts[1][0]
-            zz = (z + 4) % NZ
-            dst[zz // 2, :, h, zz % 2, :n, :] = jnp.zeros((2, n, 256), F32)
-
-    def half_copy(m):
+        parts = []
+        for role in range(2):
+            if rows == 16:
+                left = ra[m, role].reshape(256, C)
+            else:
+                left = ra3[role].astype(F32).reshape(rows * 16, C).astype(BF)
+            part = lax.dot_general(
+                left, rw[role, cn, h].reshape(256, C), contract, preferred_element_type=F32)
+            parts.append(part.reshape(4, 2, n, 256))
+        for role in range(2):
+            for j in range(1, 4):
+                zz = source(role, j)
+                dst[zz // 2, :, h, zz % 2, :n, :] = parts[role][j]
+        dst[z // 2, :, h, z % 2, :n, :] = parts[0][0] + parts[1][0]
+        zz = (z + 4) % NZ
+        dst[zz // 2, :, h, zz % 2, :n, :] = jnp.zeros((2, n, 256), F32)
+
+    def half_copy(m, h):
         n = A_CHUNKS[m][1] * 2
         return pltpu.make_async_remote_copy(
-            src_ref=half.at[:, :, :, :, pl.ds(0, n)], dst_ref=r1.at[m, :, :, :, :, pl.ds(0, n)],
-            send_sem=s0s.at[m], recv_sem=s0r.at[m],
+            src_ref=half.at[:, :, h, :, pl.ds(0, n)], dst_ref=r1.at[m, :, :, h, :, pl.ds(0, n)],
+            send_sem=s0s.at[m, h], recv_sem=s0r.at[m, h],
             device_id=device(x, y, z, 1 - c), device_id_type=MESH)
 
     def xy_copy(m, off):
@@ -248,65 +243,107 @@
             send_sem=s1s.at[m, off - 1], recv_sem=s1r.at[m, off - 1],
             device_id=device(xd, yd, z, c), device_id_type=MESH)
 
-    def zr_copy(g, j):
+    def zr_copy(m, j):
+        n = A_CHUNKS[m][1]
         off = far_first(j)
         zd = (z + off) % NZ
         return pltpu.make_async_remote_copy(
-            src_ref=zb.at[g, zd], dst_ref=zr.at[g, off - 1],
-            send_sem=s3s.at[g, off - 1], recv_sem=s3r.at[g, off - 1],
+            src_ref=zb.at[m, zd, pl.ds(0, n)], dst_ref=zr.at[m, off - 1, pl.ds(0, n)],
+            send_sem=s3s.at[m, off - 1], recv_sem=s3r.at[m, off - 1],
             device_id=device(x, y, zd, c), device_id_type=MESH)
 
     def pair_stage(m):
         n = A_CHUNKS[m][1] * 2
         if m > 0:
-            half_copy(m - 1).wait_send()
-        multiply(m, 1 - c, half)
-        half_copy(m).start()
-        multiply(m, c, own)
-        half_copy(m).wait_recv()
-        for d in (2, 1, 3, 0):
-            xd = (x + d) % NX
-            r1[m, xd, :, :, :, :n] = r1[m, xd, :, :, :, :n] + own[xd, :, :, :, :n]
-
-            @pl.loop(0 if d > 0 else 1, NY)
-            def _(j):
-                xy_copy(m, d * NY + j).start()
-
-    def gathered(m):
-        n = A_CHUNKS[m][1] * 2
+            for h in range(2):
+                half_copy(m - 1, h).wait_send()
+
+        @pl.loop(0, 2)
+        def _(h):
+            multiply(m, 1 - c, half, h)
+            half_copy(m, h).start()
+
+        @pl.loop(0, 2)
+        def _(h):
+            multiply(m, c, own, h)
+
+        @pl.loop(0, 2)
+        def _(h):
+            half_copy(m, h).wait_recv()
+            for d in (2, 1, 3, 0):
+                xd = (x + d) % NX
+                r1[m, xd, :, h, :, :n] = r1[m, xd, :, h, :, :n] + own[xd, :, h, :, :n]
+                for b in range(2):
+                    dy = (h * 2 + b - y + NY) % NY
+                    if d > 0:
+                        xy_copy(m, d * NY + dy).start()
+                    else:
+                        @pl.when(dy > 0)
+                        def _():
+                            xy_copy(m, dy).start()
+
+    def plane_stage(m):
+        n = A_CHUNKS[m][1]
 
         @pl.loop(1, NX * NY)
         def _(off):
             xy_copy(m, off).wait_recv()
 
-        total = r1[m, x, ylo, yhi, :, :n]
+        total = r1[m, x, ylo, yhi, :, :2 * n]
         for off in range(1, NX * NY):
-            total = total + xyr[m, off - 1, :, :n]
-        total = total.reshape(2 * n, 256)
-        if n < 32:
-            total = jnp.concatenate([total, jnp.zeros_like(total)], axis=0)
-        return total
-
-    def plane_stage(g):
-        both = jnp.concatenate([gathered(2 * g), gathered(2 * g + 1)], axis=0)
-        zb[g] = both.T.reshape(NZ, 32, 128)
+            total = total + xyr[m, off - 1, :, :2 * n]
+        total = total.reshape(4 * n, 256)
+        for zd in range(NZ):
+            zb[m, zd, :n] = jnp.concatenate(
+                [total[n * q:n * q + n, 32 * zd:32 * zd + 32] for q in range(4)], axis=1)
 
         @pl.loop(0, NZ - 1)
         def _(j):
-            zr_copy(g, j).start()
-
-    def last_stage(g):
+            zr_copy(m, j).start()
+
+    def last_stage(m):
+        n = A_CHUNKS[m][1]
+
         @pl.loop(0, NZ - 1)
         def _(j):
-            zr_copy(g, j).wait_recv()
-
-        final = zb[g, z]
+            zr_copy(m, j).wait_recv()
+
+        final = zb[m, z, :n]
         for d in range(1, NZ):
-            final = final + zr[g, d - 1]
-        out0[g] = final
-
-    load(0).start()
+            final = final + zr[m, d - 1, :n]
+        return final
+
+    def finish():
+        for cp in small_loads:
+            cp.wait()
+        finals = [last_stage(m) for m in range(na)]
+        cycle = jnp.concatenate(
+            [finals[m][:, 32 * q:32 * q + 32] for q in range(4) for m in range(na)], axis=0).T
+        lane = lax.broadcasted_iota(jnp.int32, (32, SLAB), 1)
+        line = lax.broadcasted_iota(jnp.int32, (32, SLAB), 0)
+        wanted = lane == (col % 4) * 32 + line
+        slab_col = jnp.sum(jnp.where(wanted, slab_v[...], 0.0), axis=1, keepdims=True)
+        which = lax.broadcasted_iota(jnp.int32, (1, JWIN), 1) == col // 4
+        pair_col = jnp.sum(jnp.where(which, pair_v[...], 0.0), axis=1, keepdims=True)
+        denom = vir_v[...] + (slab_col - pair_col)
+        out[...] = (res_v[...] + cycle) / denom
+
+    for h in range(2):
+        first_load(h).start()
+    barrier = pltpu.get_barrier_semaphore()
+    for off in range(1, NX * NY):
+        peer = device((x + off // NY) % NX, (y + off % NY) % NY, z, c)
+        pl.semaphore_signal(barrier, inc=1, device_id=peer, device_id_type=MESH)
+    for d in range(1, NZ):
+        for cd in range(NC):
+            pl.semaphore_signal(barrier, inc=1, device_id=device(x, y, (z + d) % NZ, cd), device_id_type=MESH)
+    pl.semaphore_signal(barrier, inc=1, device_id=device(x, y, z, 1 - c), device_id_type=MESH)
     load(1).start()
+    small_loads = [
+        pltpu.make_async_copy(src, dst, small_sem.at[i])
+        for i, (src, dst) in enumerate(((residual, res_v), (vir, vir_v), (slab, slab_v), (pair, pair_v)))]
+    for cp in small_loads:
+        cp.start()
     perm[...] = permutation(16)
     perm3[...] = permutation(8)
 
@@ -337,23 +374,24 @@
     plane_stage(0)
     arrived(4)
     pair_stage(2)
+    plane_stage(1)
     arrived(5)
     pair_stage(3)
-    plane_stage(1)
-    last_stage(0)
-    last_stage(1)
-
+    plane_stage(2)
+    plane_stage(3)
+    finish()
     sent(4)
     sent(5)
-    half_copy(na - 1).wait_send()
+    for h in range(2):
+        half_copy(na - 1, h).wait_send()
     for m in range(na):
         @pl.loop(1, NX * NY)
         def _(off):
             xy_copy(m, off).wait_send()
-    for g in range(na // 2):
+    for m in range(na):
         @pl.loop(0, NZ - 1)
         def _(j):
-            zr_copy(g, j).wait_send()
+            zr_copy(m, j).wait_send()
     for i in range(nw):
         @pl.loop(0, 4)
         def _(j):
@@ -370,10 +408,10 @@
 def body(ampl, integrals, residual_in, vir_energy, slab_energy, pair_energy):
     DMA = pltpu.SemaphoreType.DMA
     nw, na = len(W_CHUNKS), len(A_CHUNKS)
-    parts = pl.pallas_call(
+    update = pl.pallas_call(
         kernel,
-        out_shape=jax.ShapeDtypeStruct((na // 2, 32, 128), F32),
-        in_specs=[pl.BlockSpec(memory_space=pl.ANY)] * 2,
+        out_shape=jax.ShapeDtypeStruct((32, 224), F32),
+        in_specs=[pl.BlockSpec(memory_space=pl.ANY)] * 6,
         out_specs=pl.BlockSpec(memory_space=pltpu.VMEM),
         scratch_shapes=[
             pltpu.VMEM((2, 16, 32, C), BF),
@@ -393,36 +431,27 @@
             pltpu.VMEM((NX, 2, 2, 2, 32, 256), F32),
             pltpu.VMEM((na, NX, 2, 2, 2, 32, 256), F32),
             pltpu.VMEM((na, NX * NY - 1, 2, 32, 256), F32),
-            pltpu.VMEM((na // 2, NZ, 32, 128), F32),
-            pltpu.VMEM((na // 2, NZ - 1, 32, 128), F32),
-            DMA((2,)),
+            pltpu.VMEM((na, NZ, 16, 128), F32),
+            pltpu.VMEM((na, NZ - 1, 16, 128), F32),
+            pltpu.VMEM((32, 224), F32),
+            pltpu.VMEM((1, 224), F32),
+            pltpu.VMEM((1, SLAB), F32),
+            pltpu.VMEM((1, JWIN), F32),
+            DMA((2,)), DMA((2,)), DMA((4,)),
             DMA((nw + na, 2, NZ)), DMA((nw + na, 2, NZ)),
             DMA((nw + na, 2, 4, NC)), DMA((nw + na, 2, 4, NC)),
             DMA((nw, 2, 4, NC)), DMA((nw, 2, 4, NC)),
             DMA((nw + na, 2)),
-            DMA((na,)), DMA((na,)),
+            DMA((na, 2)), DMA((na, 2)),
             DMA((na, NX * NY - 1)), DMA((na, NX * NY - 1)),
-            DMA((na // 2, NZ - 1)), DMA((na // 2, NZ - 1)),
+            DMA((na, NZ - 1)), DMA((na, NZ - 1)),
         ],
         compiler_params=pltpu.CompilerParams(
             collective_id=0, has_side_effects=True, vmem_limit_bytes=60 * 1024 * 1024),
         cost_estimate=pl.CostEstimate(flops=2 * 1792 * 1024 * 1792, bytes_accessed=10 * 1024 * 1024, transcendentals=0),
         name="cycle",
-    )(ampl, integrals)
-    pieces = [
-        parts[m // 2, :, m % 2 * 64:m % 2 * 64 + 4 * n].reshape(32, 4, n) for m, (_, n) in enumerate(A_CHUNKS)]
-    cycle = jnp.concatenate(pieces, axis=2).reshape(32, 224).T
-
-    local_cols = cycle.shape[1]
-    columns = lax.axis_index("col") * local_cols + jnp.arange(local_cols, dtype=jnp.int32)
-    slab_index = columns % SLAB
-    occ_index = columns // SLAB
-    slab_local = jnp.sum(
-        jnp.where(slab_index[:, None] == jnp.arange(SLAB, dtype=jnp.int32)[None, :], slab_energy[None, :], 0.0), axis=1)
-    pair_local = jnp.sum(
-        jnp.where(occ_index[:, None] == jnp.arange(JWIN, dtype=jnp.int32)[None, :], pair_energy[None, :], 0.0), axis=1)
-    denom = vir_energy[:, None] + (slab_local - pair_local)[None, :]
-    return (residual_in + cycle) / denom
+    )(ampl, integrals, residual_in.T, vir_energy[None, :], slab_energy[None, :], pair_energy[None, :])
+    return update.T
 
 
 def solution(mesh):

time: 254 us -> 249 us (0.980)
  no operation moved by 1% of the time
where the time goes in v4:
time: 249 us
  Pallas kernels  248 us (100%)
    pallas_call x1, Pallas kernels, body(): pl.pallas_call(kernel, out_shape=jax.ShapeDtypeStruct((32, 224), F32), in...  248 us

profile of v4, /device:TPU:24, one launch (start us, length us, event | category | flops | bytes accessed | tf_op | source)
XLA Modules:
  0.0 249.1 jit_solution(14902458518820871690)
XLA Ops:
  0.0 247.7 %cycle.1 = f32[32,224]{1,0:T(8,128)} custom-call(bf16[56,32,1792]{2,1,0:T(8,128)(2,1)} %ampl.1, bf16[32,32,1792]{2,1,0:T(8,128)(2,1)} %integ.1, f32[32,224]{1,0:T(8,128)} %bitcast.6, f32[1,224]{1,0:T(1,128)} %bitcast.7, f32[1,128]{1,0:T(1,128)} %bitcast.8, f32[1,8]{1,0:T(1,128)} %bitcast.9), custom_call_target="tpu_custom_call" | custom-call | flops 6576668672 | bytes 10485760 | tf_op jit(solution)/shard_map/cycle/pallas_call | solution.py:411
  247.7 1.4 copy.8

commit v5 on v4

--- a/solution.py
+++ b/solution.py
@@ -255,8 +255,7 @@
     def pair_stage(m):
         n = A_CHUNKS[m][1] * 2
         if m > 0:
-            for h in range(2):
-                half_copy(m - 1, h).wait_send()
+            half_sent(m - 1)
 
         @pl.loop(0, 2)
         def _(h):
@@ -313,20 +312,41 @@
             final = final + zr[m, d - 1, :n]
         return final
 
-    def finish():
-        for cp in small_loads:
-            cp.wait()
-        finals = [last_stage(m) for m in range(na)]
-        cycle = jnp.concatenate(
-            [finals[m][:, 32 * q:32 * q + 32] for q in range(4) for m in range(na)], axis=0).T
+    def y_sent(i):
+        for h in range(2):
+            @pl.loop(0, NZ)
+            def _(zd):
+                y_copy(i, h, zd).wait_send()
+
+    def pass_sent(i):
+        @pl.loop(0, 4)
+        def _(j):
+            for role in range(2):
+                for cc in range(NC):
+                    pass_copy(i, role, j, cc).wait_send()
+
+    def xy_sent(m):
+        @pl.loop(1, NX * NY)
+        def _(off):
+            xy_copy(m, off).wait_send()
+
+    def zr_sent(m):
+        @pl.loop(0, NZ - 1)
+        def _(j):
+            zr_copy(m, j).wait_send()
+
+    def half_sent(m):
+        for h in range(2):
+            half_copy(m, h).wait_send()
+
+    def denominators():
         lane = lax.broadcasted_iota(jnp.int32, (32, SLAB), 1)
         line = lax.broadcasted_iota(jnp.int32, (32, SLAB), 0)
         wanted = lane == (col % 4) * 32 + line
         slab_col = jnp.sum(jnp.where(wanted, slab_v[...], 0.0), axis=1, keepdims=True)
         which = lax.broadcasted_iota(jnp.int32, (1, JWIN), 1) == col // 4
         pair_col = jnp.sum(jnp.where(which, pair_v[...], 0.0), axis=1, keepdims=True)
-        denom = vir_v[...] + (slab_col - pair_col)
-        out[...] = (res_v[...] + cycle) / denom
+        return vir_v[...] + (slab_col - pair_col)
 
     for h in range(2):
         first_load(h).start()
@@ -372,37 +392,37 @@
     forward(5)
     pair_stage(1)
     plane_stage(0)
+    for i in range(nw + na):
+        y_sent(i)
+    for i in range(nw):
+        pass_sent(i)
     arrived(4)
     pair_stage(2)
     plane_stage(1)
+    xy_sent(0)
+    xy_sent(1)
+    zr_sent(0)
+    sent(4)
     arrived(5)
     pair_stage(3)
     plane_stage(2)
+    for cp in small_loads:
+        cp.wait()
+    denom = denominators()
+    finals = [last_stage(0), last_stage(1)]
+    zr_sent(1)
+    sent(5)
+    half_sent(3)
+    xy_sent(2)
     plane_stage(3)
-    finish()
-    sent(4)
-    sent(5)
-    for h in range(2):
-        half_copy(na - 1, h).wait_send()
-    for m in range(na):
-        @pl.loop(1, NX * NY)
-        def _(off):
-            xy_copy(m, off).wait_send()
-    for m in range(na):
-        @pl.loop(0, NZ - 1)
-        def _(j):
-            zr_copy(m, j).wait_send()
-    for i in range(nw):
-        @pl.loop(0, 4)
-        def _(j):
-            for role in range(2):
-                for cc in range(NC):
-                    pass_copy(i, role, j, cc).wait_send()
-    for i in range(nw + na):
-        for h in range(2):
-            @pl.loop(0, NZ)
-            def _(zd):
-                y_copy(i, h, zd).wait_send()
+    finals.append(last_stage(2))
+    zr_sent(2)
+    xy_sent(3)
+    finals.append(last_stage(3))
+    cycle = jnp.concatenate(
+        [finals[m][:, 32 * q:32 * q + 32] for q in range(4) for m in range(na)], axis=0).T
+    out[...] = (res_v[...] + cycle) / denom
+    zr_sent(3)
 
 
 def body(ampl, integrals, residual_in, vir_energy, slab_energy, pair_energy):

time: 249 us -> 248 us (level)
  no operation moved by 1% of the time
where the time goes in v5:
time: 248 us; the launch traced here: 247 us
  Pallas kernels  246 us (99%)
    pallas_call x1, Pallas kernels, body(): pl.pallas_call(kernel, out_shape=jax.ShapeDtypeStruct((32, 224), F32), in...  246 us

profile of v5, /device:TPU:24, one launch (start us, length us, event | category | flops | bytes accessed | tf_op | source)
XLA Modules:
  0.0 247.4 jit_solution(7888674226370049945)
XLA Ops:
  0.0 246.0 %cycle.1 = f32[32,224]{1,0:T(8,128)} custom-call(bf16[56,32,1792]{2,1,0:T(8,128)(2,1)} %ampl.1, bf16[32,32,1792]{2,1,0:T(8,128)(2,1)} %integ.1, f32[32,224]{1,0:T(8,128)} %bitcast.6, f32[1,224]{1,0:T(1,128)} %bitcast.7, f32[1,128]{1,0:T(1,128)} %bitcast.8, f32[1,8]{1,0:T(1,128)} %bitcast.9), custom_call_target="tpu_custom_call" | custom-call | flops 6576668672 | bytes 10485760 | tf_op jit(solution)/shard_map/cycle/pallas_call | solution.py:431
  246.1 1.4 copy.8

commit v6 on v5

--- a/solution.py
+++ b/solution.py
@@ -421,7 +421,8 @@
     finals.append(last_stage(3))
     cycle = jnp.concatenate(
         [finals[m][:, 32 * q:32 * q + 32] for q in range(4) for m in range(na)], axis=0).T
-    out[...] = (res_v[...] + cycle) / denom
+    out[0] = res_v[...] + cycle
+    out[1] = denom
     zr_sent(3)
 
 
@@ -430,7 +431,7 @@
     nw, na = len(W_CHUNKS), len(A_CHUNKS)
     update = pl.pallas_call(
         kernel,
-        out_shape=jax.ShapeDtypeStruct((32, 224), F32),
+        out_shape=jax.ShapeDtypeStruct((2, 32, 224), F32),
         in_specs=[pl.BlockSpec(memory_space=pl.ANY)] * 6,
         out_specs=pl.BlockSpec(memory_space=pltpu.VMEM),
         scratch_shapes=[
@@ -471,7 +472,7 @@
         cost_estimate=pl.CostEstimate(flops=2 * 1792 * 1024 * 1792, bytes_accessed=10 * 1024 * 1024, transcendentals=0),
         name="cycle",
     )(ampl, integrals, residual_in.T, vir_energy[None, :], slab_energy[None, :], pair_energy[None, :])
-    return update.T
+    return (update[0] / update[1]).T
 
 
 def solution(mesh):

time: 248 us -> 248 us (level)
  no operation moved by 1% of the time
where the time goes in v6:
time: 248 us; the launch traced here: 247 us
  Pallas kernels  246 us (99%)
    pallas_call x1, Pallas kernels, body(): pl.pallas_call(kernel, out_shape=jax.ShapeDtypeStruct((2, 32, 224), F32),...  246 us

profile of v6, /device:TPU:24, one launch (start us, length us, event | category | flops | bytes accessed | tf_op | source)
XLA Modules:
  0.0 247.5 jit_solution(7896239275447313105)
XLA Ops:
  0.0 246.1 %cycle.1 = f32[2,32,224]{2,1,0:T(8,128)} custom-call(bf16[56,32,1792]{2,1,0:T(8,128)(2,1)} %ampl.1, bf16[32,32,1792]{2,1,0:T(8,128)(2,1)} %integ.1, f32[32,224]{1,0:T(8,128)} %bitcast.8, f32[1,224]{1,0:T(1,128)} %bitcast.9, f32[1,128]{1,0:T(1,128)} %bitcast.10, f32[1,8]{1,0:T(1,128)} %bitcast.11), custom_call_target="tpu_custom_call" | custom-call | flops 6576668672 | bytes 10485760 | tf_op jit(solution)/shard_map/cycle/pallas_call | solution.py:432
  246.1 1.4 divide_bitcast_fusion

commit v7 on v5

--- a/solution.py
+++ b/solution.py
@@ -265,9 +265,6 @@
         @pl.loop(0, 2)
         def _(h):
             multiply(m, c, own, h)
-
-        @pl.loop(0, 2)
-        def _(h):
             half_copy(m, h).wait_recv()
             for d in (2, 1, 3, 0):
                 xd = (x + d) % NX

time: 248 us -> 247 us (level)
  no operation moved by 1% of the time
where the time goes in v7:
time: 247 us; the launch traced here: 246 us
  Pallas kernels  244 us (99%)
    pallas_call x1, Pallas kernels, body(): pl.pallas_call(kernel, out_shape=jax.ShapeDtypeStruct((32, 224), F32), in...  244 us

profile of v7, /device:TPU:24, one launch (start us, length us, event | category | flops | bytes accessed | tf_op | source)
XLA Modules:
  0.0 245.8 jit_solution(4032563968521803751)
XLA Ops:
  0.0 244.4 %cycle.1 = f32[32,224]{1,0:T(8,128)} custom-call(bf16[56,32,1792]{2,1,0:T(8,128)(2,1)} %ampl.1, bf16[32,32,1792]{2,1,0:T(8,128)(2,1)} %integ.1, f32[32,224]{1,0:T(8,128)} %bitcast.6, f32[1,224]{1,0:T(1,128)} %bitcast.7, f32[1,128]{1,0:T(1,128)} %bitcast.8, f32[1,8]{1,0:T(1,128)} %bitcast.9), custom_call_target="tpu_custom_call" | custom-call | flops 6576668672 | bytes 10485760 | tf_op jit(solution)/shard_map/cycle/pallas_call | solution.py:428
  244.4 1.4 copy.8
